TPU v7x, 32 devices: a whole 2x2x4 slice. The times are simulated.
32 devices in a mesh: blk: 16 (over z, y, core), group: 2 (over x).
Axes of the slice: x: 2, y: 2, z: 4, core: 2. Of those that a mesh axis runs over, the one named last changes fastest.
Arguments:
- image_feats: bfloat16 [4096, 768], P(('blk', 'group')), may hold values from -0.796875 to 0.796875
- text_feats: bfloat16 [4096, 768], P(('blk', 'group')), may hold values from -0.796875 to 0.796875
- image_proj: bfloat16 [768, 768], replicated, may hold values from -0.21875 to 0.21875
- text_proj: bfloat16 [768, 768], replicated, may hold values from -0.21875 to 0.21875
- logit_scale: float32 [1], replicated, may hold values from 5 to 20
- logit_bias: float32 [1], replicated, may hold values from -3 to 0
- match: int32 [4096], P(('blk', 'group')), may hold values from 0 to 4095, as said below
Outputs:
- grad_image_feats: bfloat16 [4096, 768], P(('blk', 'group'))
- grad_text_feats: bfloat16 [4096, 768], P(('blk', 'group'))
Inputs may be any that keep to these rules, and one draw needn't show every extreme that they name: match of an image row in block b (rows b * 2 * 128 to (b + 1) * 2 * 128 - 1) names a report row of one of the blocks (b - k) mod 16, k below 4.
All inputs are finite; a program needn't handle non-finite values.
Results may differ from a plain program's by a relative error of at most 0.02.
Values may be sent and summed in bfloat16 or wider, within the bound.
A program may use at most 64 MiB of HBM per device.

v0:
```python
import functools

import jax
import jax.numpy as jnp
from jax import lax
from jax.experimental import pallas as pl
from jax.experimental.pallas import tpu as pltpu
from jax.sharding import PartitionSpec as P

MESH = pl.DeviceIdType.MESH
SPAN = 4
OWN, AT_A, AT_C, AT_B = range(SPAN)
CHUNKS = 2
PARTS = 3
A, C, A2, C2 = range(0, 4 * CHUNKS, CHUNKS)
B, B2, X, M, X2 = range(4 * CHUNKS, 4 * CHUNKS + 5)
SEMS = 4 * CHUNKS + 5


def embed(feats, proj, loads):
    part = proj.shape[0] // PARTS
    x = 0.0
    for i, load in enumerate(loads):
        load.wait()
        here = slice(i * part, (i + 1) * part)
        x = x + jnp.dot(feats[:, here], proj[here, :], preferred_element_type=jnp.float32)
    inv = lax.rsqrt(jnp.sum(x * x, axis=-1, keepdims=True) + 1e-06)
    return x * inv, inv


def back_norm(grad, unit, inv, turned):
    inner = jnp.sum(grad * unit, axis=-1, keepdims=True)
    grad_x = (inv * (grad - inner * unit)).astype(jnp.bfloat16)
    out = jnp.dot(grad_x, turned, preferred_element_type=jnp.float32)
    return out.astype(jnp.bfloat16)


def kernel(
    n,
    image_feats, text_feats, image_proj, text_proj, matches, scale_ref, bias_ref,
    out,
    feats_i, feats_t, proj_i, proj_t, turned_i, turned_t,
    unit_i, inv_i, unit_t, inv_t, images, images_turned, texts, coefs, match, match_nbr,
    gi_own, gt_own, gt_a, send_a, send_b, send_c, send_x,
    got_a, got_b, got_c, got_x,
    load_sem, send_sem, recv_sem,
):
    rows = match.shape[1]
    step = rows // CHUNKS
    blk = lax.axis_index("blk")
    grp = lax.axis_index("group")
    odd = lax.rem(blk, 2)

    def at(distance):
        return lax.rem(blk + distance + n, n)

    sibling = blk + 1 - 2 * odd
    across = (blk, 1 - grp)
    from_a, from_b, from_c = at(-2), at(2 * odd - 3), at(-1 - 2 * odd)

    def load(src, dst, sem):
        return pltpu.make_async_copy(src, dst, load_sem.at[sem])

    def load_parts(src, dst, sem):
        part = src.shape[0] // PARTS
        return [
            load(src.at[pl.ds(i * part, part)], dst.at[pl.ds(i * part, part)], sem + i)
            for i in range(PARTS)
        ]

    def start(copies):
        for copy in copies:
            copy.start()

    load_t = load(text_feats, feats_t, 0)
    load_i = load(image_feats, feats_i, 1)
    load_m = load(matches, match, 2)
    loads_t = load_parts(text_proj, proj_t, 3)
    loads_i = load_parts(image_proj, proj_i, 3 + PARTS)
    load_t.start()
    start(loads_t)
    load_i.start()
    start(loads_i)
    load_m.start()

    barrier = pltpu.get_barrier_semaphore()

    def greet(partner):
        pl.semaphore_signal(barrier, inc=1, device_id=partner, device_id_type=MESH)

    greet((sibling, grp))
    greet(across)
    greet((at(6 * odd - 3), grp))
    greet((at(2), grp))
    greet((at(-2), grp))

    def remote(role, src, dst, partner):
        return pltpu.make_async_remote_copy(
            src_ref=src, dst_ref=dst, send_sem=send_sem.at[role],
            recv_sem=recv_sem.at[role], device_id=partner, device_id_type=MESH,
        )

    def part(i):
        return pl.ds(i * step, step)

    def between(role, src, dst, partner):
        return [
            remote(role + i, src.at[part(i)], dst.at[part(i)], partner)
            for i in range(CHUNKS)
        ]

    def wait_recv(copies):
        for copy in copies:
            copy.wait_recv()

    def wait_send(copies):
        for copy in copies:
            copy.wait_send()

    def slot(place):
        return texts.at[pl.ds(place * rows, rows)]

    load_t.wait()
    unit, inv = embed(feats_t, proj_t, loads_t)
    texts[:rows, :] = unit.astype(jnp.bfloat16)

    pl.semaphore_wait(barrier, 5)
    copy_a = between(A, slot(OWN), slot(AT_A), (at(2), grp))
    copy_b = remote(B, slot(OWN), slot(AT_B), (at(1 + 2 * odd), grp))
    copy_c = between(C, slot(AT_A), slot(AT_C), (sibling, grp))
    copy_m = remote(M, match, match_nbr, across)
    start(copy_a)
    pl.when(odd == 0)(copy_b.start)
    load_m.wait()
    copy_m.start()
    unit_t[...] = unit
    inv_t[...] = inv

    load_i.wait()
    unit, inv = embed(feats_i, proj_i, loads_i)
    images[:rows, :] = unit.astype(jnp.bfloat16)
    copy_x = remote(X, images.at[pl.ds(0, rows)], images.at[pl.ds(rows, rows)], across)
    copy_x.start()
    unit_i[...] = unit
    inv_i[...] = inv

    scale = scale_ref[0]
    bias = bias_ref[0]

    def pair(place, source):
        ids = (source * 2 + grp) * rows + lax.broadcasted_iota(
            jnp.int32, (rows, 2 * rows), 0
        )
        wanted = jnp.concatenate([match[...], match_nbr[...]], axis=1)
        hit = wanted == ids
        here = slice(place * rows, (place + 1) * rows)
        logits = (
            scale
            * jnp.dot(texts[here, :], images_turned[...], preferred_element_type=jnp.float32)
            + bias
        )
        weight = jax.nn.sigmoid(jnp.where(hit, -logits, logits)) * scale
        coef = jnp.where(hit, -weight, weight).astype(jnp.bfloat16)
        coefs[here, :] = coef
        return jnp.dot(coef, images[...], preferred_element_type=jnp.float32)

    def image_grad(which):
        return lax.dot_general(
            coefs[:, which], texts[...], (((0,), (0,)), ((), ())),
            preferred_element_type=jnp.float32,
        )

    back_a = between(A2, send_a, got_a, (from_a, grp))
    back_b = remote(B2, send_b, got_b, (from_b, grp))
    back_c = between(C2, send_c, got_c, (sibling, grp))
    back_x = remote(X2, send_x, got_x, across)

    def pass_on(come, go):
        for i in range(CHUNKS):
            come[i].wait_recv()
            go[i].start()

    def finish_b():
        copy_b.wait_recv()
        send_b[...] = pair(AT_B, from_b).astype(jnp.bfloat16)
        back_b.start()

    def late_b():
        wait_send(copy_a)
        copy_b.start()

    pl.when(odd == 1)(late_b)
    pass_on(copy_a, copy_c)
    copy_m.wait()
    copy_x.wait()
    images_turned[...] = images[...].T
    pl.when(odd == 1)(finish_b)
    gt_a[...] = pair(AT_A, from_a)
    gt_own[...] = pair(OWN, blk)

    wait_recv(copy_c)
    send_c[...] = pair(AT_C, from_c).astype(jnp.bfloat16)
    start(back_c)
    pl.when(odd == 0)(finish_b)

    for i in range(CHUNKS):
        back_c[i].wait_recv()
        send_a[part(i), :] = (
            gt_a[part(i), :] + got_c[part(i), :].astype(jnp.float32)
        ).astype(jnp.bfloat16)
        back_a[i].start()

    send_x[...] = image_grad(slice(rows, 2 * rows)).astype(jnp.bfloat16)
    back_x.start()
    turned_i[...] = proj_i[...].T
    turned_t[...] = proj_t[...].T
    gi_own[...] = image_grad(slice(0, rows))

    def finish_image():
        back_x.wait_recv()
        grad = gi_own[...] + got_x[...].astype(jnp.float32)
        out[:rows, :] = back_norm(grad, unit_i[...], inv_i[...], turned_i[...])

    def finish_text():
        back_b.wait_recv()
        gt_own[...] += got_b[...].astype(jnp.float32)
        wait_recv(back_a)
        grad = gt_own[...] + got_a[...].astype(jnp.float32)
        out[rows:, :] = back_norm(grad, unit_t[...], inv_t[...], turned_t[...])

    pl.when(blk < 2)(finish_text)
    finish_image()
    pl.when(blk >= 2)(finish_text)

    pl.when(odd == 0)(lambda: wait_send(copy_a))
    for copies in ([copy_b], copy_c, back_a, [back_b], back_c, [back_x]):
        wait_send(copies)


def body(image_feats, text_feats, image_proj, text_proj, logit_scale, logit_bias, match):
    n = lax.axis_size("blk")
    rows, depth = image_feats.shape
    half = lambda *shape: pltpu.VMEM(shape, jnp.bfloat16)
    full = lambda *shape: pltpu.VMEM(shape, jnp.float32)
    far = pl.BlockSpec(memory_space=pltpu.HBM)
    near = pl.BlockSpec(memory_space=pltpu.VMEM)
    scalar = pl.BlockSpec(memory_space=pltpu.SMEM)
    tile = (rows, depth)
    both = pl.pallas_call(
        functools.partial(kernel, n),
        out_shape=jax.ShapeDtypeStruct((2 * rows, depth), jnp.bfloat16),
        in_specs=[far] * 5 + [scalar] * 2,
        out_specs=near,
        scratch_shapes=[
            half(*tile), half(*tile), half(depth, depth), half(depth, depth),
            half(depth, depth), half(depth, depth),
            full(*tile), full(rows, 1), full(*tile), full(rows, 1),
            half(2 * rows, depth), half(depth, 2 * rows),
            half(SPAN * rows, depth), half(SPAN * rows, 2 * rows),
            pltpu.VMEM((1, rows), jnp.int32), pltpu.VMEM((1, rows), jnp.int32),
            full(*tile), full(*tile), full(*tile),
            half(*tile), half(*tile), half(*tile), half(*tile),
            half(*tile), half(*tile), half(*tile), half(*tile),
            pltpu.SemaphoreType.DMA((3 + 2 * PARTS,)),
            pltpu.SemaphoreType.DMA((SEMS,)),
            pltpu.SemaphoreType.DMA((SEMS,)),
        ],
        compiler_params=pltpu.CompilerParams(
            collective_id=0, has_side_effects=True, vmem_limit_bytes=32 * 1024 * 1024
        ),
        cost_estimate=pl.CostEstimate(
            flops=8 * rows * depth * depth + 48 * rows * rows * depth,
            bytes_accessed=4 * depth * depth + 8 * rows * depth,
            transcendentals=8 * rows * rows,
        ),
    )(
        *(
            pltpu.with_memory_space_constraint(x, pltpu.HBM)
            for x in (image_feats, text_feats, image_proj, text_proj, match.reshape(1, rows))
        ),
        logit_scale, logit_bias,
    )
    return both[:rows], both[rows:]


def solution(mesh):
    rows = P(("blk", "group"), None)
    return jax.shard_map(
        body,
        mesh=mesh,
        in_specs=(rows, rows, P(), P(), P(), P(), P(("blk", "group"))),
        out_specs=(rows, rows),
        check_vma=False,
    )
```

profile of v0, /device:TPU:0, one launch (start us, length us, event | category | flops | bytes accessed | tf_op | source)
XLA Modules:
  0.0 26.0 jit_solution(6165919955359549632)
XLA Ops:
  1.9 23.3 %shard_map.86 = bf16[256,768]{1,0:T(8,128)(2,1)S(1)} custom-call(bf16[128,768]{1,0:T(8,128)(2,1)} %image_feats.1, bf16[128,768]{1,0:T(8,128)(2,1)} %text_feats.1, bf16[768,768]{1,0:T(8,128)(2,1)} %image_proj.1, bf16[768,768]{1,0:T(8,128)(2,1)} %text_proj.1, s32[1,128]{1,0:T(1,128)} %bitcast.1, f32[1]{0:T(128)S(6)} %copy.9.scale_ref, f32[1]{0:T(128)S(6)} %copy.10.bias_ref), custom_call_target="tpu_custom_call" | custom-call | flops 1207959552 | bytes 3145728 | tf_op jit(solution)/shard_map/pallas_call | solution.py:249
  25.2 0.8 %fusion = (bf16[128,768]{1,0:T(8,128)(2,1)}, bf16[128,768]{1,0:T(8,128)(2,1)}) fusion(bf16[256,768]{1,0:T(8,128)(2,1)S(1)} %shard_map.86), kind=kLoop, calls=%fused_computation | loop fusion | bytes 786432 | tf_op jit(solution)/shard_map/slice | solution.py:283
where the time goes:
time: 26.2 us; the launch traced here: 26 us
  Pallas kernels  23.3 us (89%)
  between operations  1.93 us (7%)
  local copies, waits for them, and re-layouts  0.77 us (3%)
    pallas_call x1, Pallas kernels, body(): pl.pallas_call(functools.partial(kernel, n), out_shape=jax.ShapeDtypeStru...  23.3 us
    slice x1, local copies, waits for them, and re-layouts, body(): return (both[:rows], both[rows:])  0.77 us

commit v1 on v0

--- a/solution.py
+++ b/solution.py
@@ -41,7 +41,7 @@
     out,
     feats_i, feats_t, proj_i, proj_t, turned_i, turned_t,
     unit_i, inv_i, unit_t, inv_t, images, images_turned, texts, coefs, match, match_nbr,
-    gi_own, gt_own, gt_a, send_a, send_b, send_c, send_x,
+    gi, gt_own, gt_a, send_a, send_b, send_c, send_x,
     got_a, got_b, got_c, got_x,
     load_sem, send_sem, recv_sem,
 ):
@@ -50,6 +50,7 @@
     blk = lax.axis_index("blk")
     grp = lax.axis_index("group")
     odd = lax.rem(blk, 2)
+    q = lax.rem(blk, 4)
 
     def at(distance):
         return lax.rem(blk + distance + n, n)
@@ -164,9 +165,9 @@
         coefs[here, :] = coef
         return jnp.dot(coef, images[...], preferred_element_type=jnp.float32)
 
-    def image_grad(which):
+    def image_grad(here):
         return lax.dot_general(
-            coefs[:, which], texts[...], (((0,), (0,)), ((), ())),
+            coefs[here, :], texts[here, :], (((0,), (0,)), ((), ())),
             preferred_element_type=jnp.float32,
         )
 
@@ -201,7 +202,8 @@
     wait_recv(copy_c)
     send_c[...] = pair(AT_C, from_c).astype(jnp.bfloat16)
     start(back_c)
-    pl.when(odd == 0)(finish_b)
+    gi[...] = image_grad(slice(0, AT_B * rows))
+    pl.when(q == 2)(finish_b)
 
     for i in range(CHUNKS):
         back_c[i].wait_recv()
@@ -210,15 +212,17 @@
         ).astype(jnp.bfloat16)
         back_a[i].start()
 
-    send_x[...] = image_grad(slice(rows, 2 * rows)).astype(jnp.bfloat16)
+    pl.when(q == 0)(finish_b)
+
+    gi[...] += image_grad(slice(AT_B * rows, SPAN * rows))
+    send_x[...] = gi[rows:, :].astype(jnp.bfloat16)
     back_x.start()
     turned_i[...] = proj_i[...].T
     turned_t[...] = proj_t[...].T
-    gi_own[...] = image_grad(slice(0, rows))
 
     def finish_image():
         back_x.wait_recv()
-        grad = gi_own[...] + got_x[...].astype(jnp.float32)
+        grad = gi[:rows, :] + got_x[...].astype(jnp.float32)
         out[:rows, :] = back_norm(grad, unit_i[...], inv_i[...], turned_i[...])
 
     def finish_text():
@@ -258,7 +262,7 @@
             half(2 * rows, depth), half(depth, 2 * rows),
             half(SPAN * rows, depth), half(SPAN * rows, 2 * rows),
             pltpu.VMEM((1, rows), jnp.int32), pltpu.VMEM((1, rows), jnp.int32),
-            full(*tile), full(*tile), full(*tile),
+            full(2 * rows, depth), full(*tile), full(*tile),
             half(*tile), half(*tile), half(*tile), half(*tile),
             half(*tile), half(*tile), half(*tile), half(*tile),
             pltpu.SemaphoreType.DMA((3 + 2 * PARTS,)),

time: 26.2 us -> 26.3 us (level)
  no operation moved by 1% of the time
where the time goes in v1:
time: 26.3 us; the launch traced here: 25.9 us
  Pallas kernels  23.2 us (88%)
  between operations  1.93 us (7%)
  local copies, waits for them, and re-layouts  0.77 us (3%)
    pallas_call x1, Pallas kernels, body(): pl.pallas_call(functools.partial(kernel, n), out_shape=jax.ShapeDtypeStru...  23.2 us
    slice x1, local copies, waits for them, and re-layouts, body(): return (both[:rows], both[rows:])  0.77 us

profile of v1, /device:TPU:0, one launch (start us, length us, event | category | flops | bytes accessed | tf_op | source)
XLA Modules:
  0.0 25.9 jit_solution(10814722593787798826)
XLA Ops:
  1.9 23.2 %shard_map.86 = bf16[256,768]{1,0:T(8,128)(2,1)S(1)} custom-call(bf16[128,768]{1,0:T(8,128)(2,1)} %image_feats.1, bf16[128,768]{1,0:T(8,128)(2,1)} %text_feats.1, bf16[768,768]{1,0:T(8,128)(2,1)} %image_proj.1, bf16[768,768]{1,0:T(8,128)(2,1)} %text_proj.1, s32[1,128]{1,0:T(1,128)} %bitcast.1, f32[1]{0:T(128)S(6)} %copy.9.scale_ref, f32[1]{0:T(128)S(6)} %copy.10.bias_ref), custom_call_target="tpu_custom_call" | custom-call | flops 1207959552 | bytes 3145728 | tf_op jit(solution)/shard_map/pallas_call | solution.py:253
  25.2 0.8 %fusion = (bf16[128,768]{1,0:T(8,128)(2,1)}, bf16[128,768]{1,0:T(8,128)(2,1)}) fusion(bf16[256,768]{1,0:T(8,128)(2,1)S(1)} %shard_map.86), kind=kLoop, calls=%fused_computation | loop fusion | bytes 786432 | tf_op jit(solution)/shard_map/slice | solution.py:287

commit v2 on v1

--- a/solution.py
+++ b/solution.py
@@ -131,7 +131,7 @@
     copy_c = between(C, slot(AT_A), slot(AT_C), (sibling, grp))
     copy_m = remote(M, match, match_nbr, across)
     start(copy_a)
-    pl.when(odd == 0)(copy_b.start)
+    pl.when(q != 3)(copy_b.start)
     load_m.wait()
     copy_m.start()
     unit_t[...] = unit
@@ -165,11 +165,13 @@
         coefs[here, :] = coef
         return jnp.dot(coef, images[...], preferred_element_type=jnp.float32)
 
-    def image_grad(here):
-        return lax.dot_general(
-            coefs[here, :], texts[here, :], (((0,), (0,)), ((), ())),
+    def image_terms():
+        gi[...] = lax.dot_general(
+            coefs[...], texts[...], (((0,), (0,)), ((), ())),
             preferred_element_type=jnp.float32,
         )
+        send_x[...] = gi[rows:, :].astype(jnp.bfloat16)
+        back_x.start()
 
     back_a = between(A2, send_a, got_a, (from_a, grp))
     back_b = remote(B2, send_b, got_b, (from_b, grp))
@@ -190,7 +192,7 @@
         wait_send(copy_a)
         copy_b.start()
 
-    pl.when(odd == 1)(late_b)
+    pl.when(q == 3)(late_b)
     pass_on(copy_a, copy_c)
     copy_m.wait()
     copy_x.wait()
@@ -202,8 +204,8 @@
     wait_recv(copy_c)
     send_c[...] = pair(AT_C, from_c).astype(jnp.bfloat16)
     start(back_c)
-    gi[...] = image_grad(slice(0, AT_B * rows))
-    pl.when(q == 2)(finish_b)
+    pl.when(odd == 0)(finish_b)
+    pl.when(odd == 1)(image_terms)
 
     for i in range(CHUNKS):
         back_c[i].wait_recv()
@@ -212,11 +214,7 @@
         ).astype(jnp.bfloat16)
         back_a[i].start()
 
-    pl.when(q == 0)(finish_b)
-
-    gi[...] += image_grad(slice(AT_B * rows, SPAN * rows))
-    send_x[...] = gi[rows:, :].astype(jnp.bfloat16)
-    back_x.start()
+    pl.when(odd == 0)(image_terms)
     turned_i[...] = proj_i[...].T
     turned_t[...] = proj_t[...].T
 
@@ -236,7 +234,7 @@
     finish_image()
     pl.when(blk >= 2)(finish_text)
 
-    pl.when(odd == 0)(lambda: wait_send(copy_a))
+    pl.when(q != 3)(lambda: wait_send(copy_a))
     for copies in ([copy_b], copy_c, back_a, [back_b], back_c, [back_x]):
         wait_send(copies)
 

time: 26.3 us -> 25.4 us (0.966)
  Pallas kernels: 23.2 us -> 22.5 us
    pallas_call x1, Pallas kernels: 23.2 us -> 22.5 us  [body(): pl.pallas_call(functools.partial(kernel, n), out_shape=jax.ShapeDtypeStru...]
where the time goes in v2:
time: 25.4 us; the launch traced here: 25.2 us
  Pallas kernels  22.5 us (89%)
  between operations  1.93 us (8%)
  local copies, waits for them, and re-layouts  0.77 us (3%)
    pallas_call x1, Pallas kernels, body(): pl.pallas_call(functools.partial(kernel, n), out_shape=jax.ShapeDtypeStru...  22.5 us
    slice x1, local copies, waits for them, and re-layouts, body(): return (both[:rows], both[rows:])  0.77 us

profile of v2, /device:TPU:0, one launch (start us, length us, event | category | flops | bytes accessed | tf_op | source)
XLA Modules:
  0.0 25.2 jit_solution(10020905469938993695)
XLA Ops:
  1.9 22.5 %shard_map.86 = bf16[256,768]{1,0:T(8,128)(2,1)S(1)} custom-call(bf16[128,768]{1,0:T(8,128)(2,1)} %image_feats.1, bf16[128,768]{1,0:T(8,128)(2,1)} %text_feats.1, bf16[768,768]{1,0:T(8,128)(2,1)} %image_proj.1, bf16[768,768]{1,0:T(8,128)(2,1)} %text_proj.1, s32[1,128]{1,0:T(1,128)} %bitcast.1, f32[1]{0:T(128)S(6)} %copy.9.scale_ref, f32[1]{0:T(128)S(6)} %copy.10.bias_ref), custom_call_target="tpu_custom_call" | custom-call | flops 1207959552 | bytes 3145728 | tf_op jit(solution)/shard_map/pallas_call | solution.py:251
  24.4 0.8 %fusion = (bf16[128,768]{1,0:T(8,128)(2,1)}, bf16[128,768]{1,0:T(8,128)(2,1)}) fusion(bf16[256,768]{1,0:T(8,128)(2,1)S(1)} %shard_map.86), kind=kLoop, calls=%fused_computation | loop fusion | bytes 786432 | tf_op jit(solution)/shard_map/slice | solution.py:285

commit v3 on v2

--- a/solution.py
+++ b/solution.py
@@ -186,7 +186,7 @@
     def finish_b():
         copy_b.wait_recv()
         send_b[...] = pair(AT_B, from_b).astype(jnp.bfloat16)
-        back_b.start()
+        pl.when(q != 0)(back_b.start)
 
     def late_b():
         wait_send(copy_a)
@@ -214,6 +214,7 @@
         ).astype(jnp.bfloat16)
         back_a[i].start()
 
+    pl.when(q == 0)(back_b.start)
     pl.when(odd == 0)(image_terms)
     turned_i[...] = proj_i[...].T
     turned_t[...] = proj_t[...].T

time: 25.4 us -> 26.1 us (1.028)
  the two profiles are of different devices: /device:TPU:0 before, /device:TPU:1 now
where the time goes in v3:
time: 26.1 us; the launch traced here: 25.9 us
  Pallas kernels  23.2 us (89%)
  between operations  1.93 us (7%)
  local copies, waits for them, and re-layouts  0.77 us (3%)
    pallas_call x1, Pallas kernels, body(): pl.pallas_call(functools.partial(kernel, n), out_shape=jax.ShapeDtypeStru...  23.2 us
    slice x1, local copies, waits for them, and re-layouts, body(): return (both[:rows], both[rows:])  0.77 us

profile of v3, /device:TPU:1, one launch (start us, length us, event | category | flops | bytes accessed | tf_op | source)
XLA Modules:
  0.0 25.9 jit_solution(817251041459904572)
XLA Ops:
  1.9 23.2 %shard_map.86 = bf16[256,768]{1,0:T(8,128)(2,1)S(1)} custom-call(bf16[128,768]{1,0:T(8,128)(2,1)} %image_feats.1, bf16[128,768]{1,0:T(8,128)(2,1)} %text_feats.1, bf16[768,768]{1,0:T(8,128)(2,1)} %image_proj.1, bf16[768,768]{1,0:T(8,128)(2,1)} %text_proj.1, s32[1,128]{1,0:T(1,128)} %bitcast.1, f32[1]{0:T(128)S(6)} %copy.9.scale_ref, f32[1]{0:T(128)S(6)} %copy.10.bias_ref), custom_call_target="tpu_custom_call" | custom-call | flops 1207959552 | bytes 3145728 | tf_op jit(solution)/shard_map/pallas_call | solution.py:252
  25.2 0.8 %fusion = (bf16[128,768]{1,0:T(8,128)(2,1)}, bf16[128,768]{1,0:T(8,128)(2,1)}) fusion(bf16[256,768]{1,0:T(8,128)(2,1)S(1)} %shard_map.86), kind=kLoop, calls=%fused_computation | loop fusion | bytes 786432 | tf_op jit(solution)/shard_map/slice | solution.py:286

commit v4 on v2

--- a/solution.py
+++ b/solution.py
@@ -12,9 +12,9 @@
 OWN, AT_A, AT_C, AT_B = range(SPAN)
 CHUNKS = 2
 PARTS = 3
-A, C, A2, C2 = range(0, 4 * CHUNKS, CHUNKS)
-B, B2, X, M, X2 = range(4 * CHUNKS, 4 * CHUNKS + 5)
-SEMS = 4 * CHUNKS + 5
+A, C, A2, B2, C2 = range(0, 5 * CHUNKS, CHUNKS)
+B, X, M, X2 = range(5 * CHUNKS, 5 * CHUNKS + 4)
+SEMS = 5 * CHUNKS + 4
 
 
 def embed(feats, proj, loads):
@@ -174,7 +174,7 @@
         back_x.start()
 
     back_a = between(A2, send_a, got_a, (from_a, grp))
-    back_b = remote(B2, send_b, got_b, (from_b, grp))
+    back_b = between(B2, send_b, got_b, (from_b, grp))
     back_c = between(C2, send_c, got_c, (sibling, grp))
     back_x = remote(X2, send_x, got_x, across)
 
@@ -186,7 +186,8 @@
     def finish_b():
         copy_b.wait_recv()
         send_b[...] = pair(AT_B, from_b).astype(jnp.bfloat16)
-        back_b.start()
+        back_b[0].start()
+        pl.when(q != 0)(lambda: start(back_b[1:]))
 
     def late_b():
         wait_send(copy_a)
@@ -205,7 +206,7 @@
     send_c[...] = pair(AT_C, from_c).astype(jnp.bfloat16)
     start(back_c)
     pl.when(odd == 0)(finish_b)
-    pl.when(odd == 1)(image_terms)
+    image_terms()
 
     for i in range(CHUNKS):
         back_c[i].wait_recv()
@@ -214,7 +215,7 @@
         ).astype(jnp.bfloat16)
         back_a[i].start()
 
-    pl.when(odd == 0)(image_terms)
+    pl.when(q == 0)(lambda: start(back_b[1:]))
     turned_i[...] = proj_i[...].T
     turned_t[...] = proj_t[...].T
 
@@ -224,7 +225,7 @@
         out[:rows, :] = back_norm(grad, unit_i[...], inv_i[...], turned_i[...])
 
     def finish_text():
-        back_b.wait_recv()
+        wait_recv(back_b)
         gt_own[...] += got_b[...].astype(jnp.float32)
         wait_recv(back_a)
         grad = gt_own[...] + got_a[...].astype(jnp.float32)
@@ -235,7 +236,7 @@
     pl.when(blk >= 2)(finish_text)
 
     pl.when(q != 3)(lambda: wait_send(copy_a))
-    for copies in ([copy_b], copy_c, back_a, [back_b], back_c, [back_x]):
+    for copies in ([copy_b], copy_c, back_a, back_b, back_c, [back_x]):
         wait_send(copies)
 
 

time: 25.4 us -> 26 us (1.024)
  the two profiles are of different devices: /device:TPU:0 before, /device:TPU:1 now
where the time goes in v4:
time: 26 us; the launch traced here: 25.8 us
  Pallas kernels  23.1 us (89%)
  between operations  1.93 us (7%)
  local copies, waits for them, and re-layouts  0.77 us (3%)
    pallas_call x1, Pallas kernels, body(): pl.pallas_call(functools.partial(kernel, n), out_shape=jax.ShapeDtypeStru...  23.1 us
    slice x1, local copies, waits for them, and re-layouts, body(): return (both[:rows], both[rows:])  0.77 us

profile of v4, /device:TPU:1, one launch (start us, length us, event | category | flops | bytes accessed | tf_op | source)
XLA Modules:
  0.0 25.8 jit_solution(773504629464618593)
XLA Ops:
  1.9 23.1 %shard_map.86 = bf16[256,768]{1,0:T(8,128)(2,1)S(1)} custom-call(bf16[128,768]{1,0:T(8,128)(2,1)} %image_feats.1, bf16[128,768]{1,0:T(8,128)(2,1)} %text_feats.1, bf16[768,768]{1,0:T(8,128)(2,1)} %image_proj.1, bf16[768,768]{1,0:T(8,128)(2,1)} %text_proj.1, s32[1,128]{1,0:T(1,128)} %bitcast.1, f32[1]{0:T(128)S(6)} %copy.9.scale_ref, f32[1]{0:T(128)S(6)} %copy.10.bias_ref), custom_call_target="tpu_custom_call" | custom-call | flops 1207959552 | bytes 3145728 | tf_op jit(solution)/shard_map/pallas_call | solution.py:252
  25.0 0.8 %fusion = (bf16[128,768]{1,0:T(8,128)(2,1)}, bf16[128,768]{1,0:T(8,128)(2,1)}) fusion(bf16[256,768]{1,0:T(8,128)(2,1)S(1)} %shard_map.86), kind=kLoop, calls=%fused_computation | loop fusion | bytes 786432 | tf_op jit(solution)/shard_map/slice | solution.py:286
